TPU v7x, 256 devices: a whole 4x4x8 slice. The times are simulated.
256 devices in a mesh: train: 32 (over y, z), query: 8 (over x, core).
Axes of the slice: x: 4, y: 4, z: 8, core: 2. Of those that a mesh axis runs over, the one named last changes fastest.
Arguments:
- train_grads: float32 [65536, 1024], P(('train', 'query'))
- queries: float32 [2048, 1024], P('query'), may hold values from -6 to 6
Outputs:
- scores: float32 [65536, 2048], P('train', 'query')
All inputs are finite; a program needn't handle non-finite values.
Results may differ from a plain program's by a relative error of at most 0.0003.
Values sent between devices are 32-bit elements; how exact they have to be, the bound alone decides.
A program may use at most 128 MiB of HBM per device.

v0:
```python
import jax
import jax.numpy as jnp
from jax import lax
from jax.sharding import PartitionSpec as P


def precondition(fisher, queries):
    width = fisher.shape[0]
    damp = 0.1 * jnp.trace(fisher) / width
    lower = jnp.linalg.cholesky(fisher + damp * jnp.eye(width, dtype=fisher.dtype))
    middle = lax.linalg.triangular_solve(lower, queries.T, left_side=True, lower=True)
    return lax.linalg.triangular_solve(lower, middle, left_side=True, lower=True, transpose_a=True)


def gram_of(rows):
    return jnp.dot(
        rows.T, rows, precision=lax.Precision.HIGHEST, preferred_element_type=jnp.float32
    )


def local(train_grads, queries):
    width = train_grads.shape[1]
    total = train_grads.shape[0] * lax.axis_size("train") * lax.axis_size("query")
    norm_factor = jnp.sqrt(jnp.float32(width))
    operand = gram_of(train_grads)
    summed = lax.psum(operand, ("train", "query"))
    fisher = summed / total
    precond = precondition(fisher, queries)
    scores = jnp.dot(
        lax.all_gather(train_grads, "query", axis=0, tiled=True),
        precond,
        precision=lax.Precision.HIGHEST,
        preferred_element_type=jnp.float32,
    )
    return scores / norm_factor


def solution(mesh):
    in_specs = (P(("train", "query"), None), P("query", None))
    out_specs = P("train", "query")
    return jax.shard_map(local, mesh=mesh, in_specs=in_specs, out_specs=out_specs, check_vma=False)
```

profile of v0, /device:TPU:1, one launch (start us, length us, event | category | flops | bytes accessed | tf_op | source)
XLA Modules:
  0.0 680.8 jit_solution(646219809023851870)
XLA Ops:
  7.4 7.0 %fusion.96 = f32[1024,1024]{0,1:T(8,128)} fusion(f32[256,1024]{1,0:T(8,128)} %param.2), kind=kOutput, calls=%fused_computation.218 | convolution fusion | flops 3221225472 | bytes 5242880 | tf_op jit(solution)/shard_map/dot_general | solution.py:16
  15.0 287.1 %all-reduce.3.cloned.1.call-done = f32[1024,1024]{0,1:T(8,128)} async-done(((f32[1024,1024]{0,1:T(8,128)}), f32[1024,1024]{0,1:T(8,128)}) %all-reduce.3.cloned.1.call-update) | async-done | bytes 4194320 | tf_op jit(solution)/shard_map/psum | solution.py:26
  302.1 3.0 select_reduce_fusion
  305.7 5.0 select_add_fusion
  310.6 5.6 copy.4
  316.2 4.5 fusion
  322.7 11.7 %cholesky.222 = f32[128,128]{1,0:T(8,128)S(1)} custom-call(f32[128,128]{1,0:T(8,128)S(1)} %cholesky.577), custom_call_target="Cholesky" | custom-call | tf_op jit(solution)/shard_map/jit(cholesky)/cholesky | solution.py:10
  334.5 9.8 %custom-call.64 = f32[1,128,128]{1,2,0:T(8,128)S(1)} custom-call(f32[1,128,128]{2,1,0:T(8,128)S(1)} %get-tuple-element.57), custom_call_target="InvertDiagBlocksLowerTriangular" | custom-call | tf_op jit(solution)/shard_map/jit(cholesky)/cholesky | solution.py:10
  347.6 11.7 %cholesky.243 = f32[128,128]{1,0:T(8,128)S(1)} custom-call(f32[128,128]{1,0:T(8,128)S(1)} %cholesky.581), custom_call_target="Cholesky" | custom-call | tf_op jit(solution)/shard_map/jit(cholesky)/cholesky | solution.py:10
  359.9 9.8 %custom-call.65 = f32[1,128,128]{1,2,0:T(8,128)S(1)} custom-call(f32[1,128,128]{2,1,0:T(8,128)S(1)} %get-tuple-element.55), custom_call_target="InvertDiagBlocksLowerTriangular" | custom-call | tf_op jit(solution)/shard_map/jit(cholesky)/cholesky | solution.py:10
  372.8 2.4 convolution_subtract_fusion.1
  375.2 11.7 %cholesky.466 = f32[128,128]{1,0:T(8,128)S(1)} custom-call(f32[128,128]{1,0:T(8,128)S(1)} %cholesky.586), custom_call_target="Cholesky" | custom-call | tf_op jit(solution)/shard_map/jit(cholesky)/cholesky | solution.py:10
  387.7 9.8 %custom-call.66 = f32[1,128,128]{1,2,0:T(8,128)S(1)} custom-call(f32[1,128,128]{2,1,0:T(8,128)S(1)} %get-tuple-element.53), custom_call_target="InvertDiagBlocksLowerTriangular" | custom-call | tf_op jit(solution)/shard_map/jit(cholesky)/cholesky | solution.py:10
  398.7 3.3 convolution_subtract_fusion.2
  402.0 11.7 %cholesky.485 = f32[128,128]{1,0:T(8,128)S(1)} custom-call(f32[128,128]{1,0:T(8,128)S(1)} %cholesky.591), custom_call_target="Cholesky" | custom-call | tf_op jit(solution)/shard_map/jit(cholesky)/cholesky | solution.py:10
  414.6 9.8 %custom-call.67 = f32[1,128,128]{1,2,0:T(8,128)S(1)} custom-call(f32[1,128,128]{2,1,0:T(8,128)S(1)} %get-tuple-element.51), custom_call_target="InvertDiagBlocksLowerTriangular" | custom-call | tf_op jit(solution)/shard_map/jit(cholesky)/cholesky | solution.py:10
  425.5 3.2 convolution_subtract_fusion.3
  428.7 12.1 %cholesky.504 = f32[128,128]{1,0:T(8,128)S(1)} custom-call(f32[128,128]{1,0:T(8,128)S(1)} %cholesky.596), custom_call_target="Cholesky" | custom-call | tf_op jit(solution)/shard_map/jit(cholesky)/cholesky | solution.py:10
  441.5 9.8 %custom-call.68 = f32[1,128,128]{1,2,0:T(8,128)S(1)} custom-call(f32[1,128,128]{2,1,0:T(8,128)S(1)} %get-tuple-element.49), custom_call_target="InvertDiagBlocksLowerTriangular" | custom-call | tf_op jit(solution)/shard_map/jit(cholesky)/cholesky | solution.py:10
  452.5 3.1 convolution_subtract_fusion.4
  455.6 11.7 %cholesky.524 = f32[128,128]{1,0:T(8,128)S(1)} custom-call(f32[128,128]{1,0:T(8,128)S(1)} %cholesky.601), custom_call_target="Cholesky" | custom-call | tf_op jit(solution)/shard_map/jit(cholesky)/cholesky | solution.py:10
  468.1 9.8 %custom-call.69 = f32[1,128,128]{1,2,0:T(8,128)S(1)} custom-call(f32[1,128,128]{2,1,0:T(8,128)S(1)} %get-tuple-element.47), custom_call_target="InvertDiagBlocksLowerTriangular" | custom-call | tf_op jit(solution)/shard_map/jit(cholesky)/cholesky | solution.py:10
  478.9 2.8 convolution_subtract_fusion.17
  481.7 11.7 %cholesky.544 = f32[128,128]{1,0:T(8,128)S(1)} custom-call(f32[128,128]{1,0:T(8,128)S(1)} %cholesky.606), custom_call_target="Cholesky" | custom-call | tf_op jit(solution)/shard_map/jit(cholesky)/cholesky | solution.py:10
  494.2 9.8 %custom-call.70 = f32[1,128,128]{1,2,0:T(8,128)S(1)} custom-call(f32[1,128,128]{2,1,0:T(8,128)S(1)} %get-tuple-element.45), custom_call_target="InvertDiagBlocksLowerTriangular" | custom-call | tf_op jit(solution)/shard_map/jit(cholesky)/cholesky | solution.py:10
  507.1 11.7 %cholesky.562 = f32[128,128]{1,0:T(8,128)S(1)} custom-call(f32[128,128]{1,0:T(8,128)S(1)} %convolution_subtract_fusion.20), custom_call_target="Cholesky" | custom-call | tf_op jit(solution)/shard_map/jit(cholesky)/cholesky | solution.py:10
  528.5 5.0 select_select_fusion
  533.5 24.5 %while.1 = (s32[]{:T(128)}, f32[1024,1024]{0,1:T(8,128)}, s32[8,2]{0,1:T(2,128)S(1)}, f32[8,128,128]{2,1,0:T(8,128)S(1)}, s32[]{:T(128)}) while((s32[]{:T(128)}, f32[1024,1024]{0,1:T(8,128)}, s32[8,2]{0,1:T(2,128)S(1)}, f32[8,128,128]{2,1,0:T(8,128)S(1)}, s32[]{:T(128)}) %tuple.49), condition=%wide.while_cond, body=%wide.while_body.sunk | while | flops 2 | bytes 393329 | solution.py:12
  534.1 2.3 dynamic-slice.7
  546.4 2.3 dynamic-slice.7
  557.9 78.8 %custom-call.71 = f32[8,128,128]{1,2,0:T(8,128)S(1)} custom-call(f32[8,128,128]{2,1,0:T(8,128)S(1)} %get-tuple-element.12), custom_call_target="InvertDiagBlocksLowerTriangular" | custom-call | tf_op jit(solution)/shard_map/triangular_solve | solution.py:12
  655.2 15.8 %fusion.1 = f32[2048,256]{0,1:T(8,128)S(1)} fusion(f32[1024,256]{1,0:T(8,128)S(1)} %constant_dynamic-update-slice_fusion.36, f32[2048,1024]{1,0:T(8,128)} %all-gather.2.cloned.1.call-done), kind=kOutput, calls=%fused_computation.10 | convolution fusion | flops 6442975232 | bytes 11534336 | tf_op jit(solution)/shard_map/dot_general | solution.py:29
  (156 shorter events, 65.5 us)
Async XLA Ops:
  7.4 294.7 %all-reduce.3.cloned.1.call-start = ((), (), s32[]{:S(2)}) async-start(), calls=%async_computation | async-start | bytes 8388608 | tf_op jit(solution)/shard_map/psum | solution.py:26
  14.4 640.8 %all-gather.2.cloned.1.call-start = ((), (), s32[]{:S(2)}) async-start(), calls=%async_computation.1 | async-start | bytes 9437184 | tf_op jit(solution)/shard_map/all_gather | solution.py:30
  320.7 2.0 copy-start.2
  370.8 2.0 copy-start
  528.5 108.3 %copy-start.3 = (f32[256,1024]{1,0:T(8,128)S(1)}, f32[256,1024]{1,0:T(8,128)}, u32[]{:S(2)}) copy-start(f32[256,1024]{1,0:T(8,128)} %param.3) | copy-start | bytes 3145732
  636.7 6.0 copy-start.1
Sparse Core Ops, SparseCore 0:
  14.5 287.5 all-reduce.2
Sparse Core Ops, SparseCore 1:
  16.9 57.4 all-gather.1
where the time goes:
time: 686 us; the launch traced here: 681 us
  waiting for transfers between devices  288 us (42%)
  other arithmetic  263 us (38%)
  matrix products  66.5 us (10%)
  local copies, waits for them, and re-layouts  41.6 us (6%)
  between operations  21.3 us (3%)
    psum x1, waiting for transfers between devices, local(): summed = lax.psum(operand, ('train', 'query'))  287 us
    another operation x30, other arithmetic, precondition(): jnp.linalg.cholesky(fisher + damp * jnp.eye(width, dtype=fisher.dtype))  167 us
    another operation x3, other arithmetic, precondition(): lax.linalg.triangular_solve(lower, middle, left_side=True, lower=True, tr...  83.8 us
    another operation x14, matrix products, precondition(): jnp.linalg.cholesky(fisher + damp * jnp.eye(width, dtype=fisher.dtype))  25.9 us
    another operation x40, local copies, waits for them, and re-layouts  24.2 us
    dot_general x1, matrix products, local(): jnp.dot(lax.all_gather(train_grads, 'query', axis=0, tiled=True), precond...  15.8 us
  transfers between devices with their start and end apart: 2, of which 1 were waited for; matrix products, arithmetic and copies ran while one was open for 50% of the time, Pallas kernels for 0%

commit v1 on v0

v1 whole, which is shorter than its diff:
```python
import functools
import jax
import jax.numpy as jnp
from jax import lax
from jax.experimental import pallas as pl
from jax.experimental.pallas import tpu as pltpu
from jax.sharding import PartitionSpec as P

f32 = jnp.float32
bf = jnp.bfloat16
B = 128
NB = 8
K = B * NB
NY, NZ, NX = 4, 8, 4
MESH = pl.DeviceIdType.MESH
OFF = [sum((NB - i) * B for i in range(k)) for k in range(NB + 1)]
CHUNKS = [(0, 1024), (1024, 1024), (2048, 1024), (3072, 1024), (4096, 512)]
STAGES = 8
NCOPY = 25 * len(CHUNKS) + 12


def split(x, n=3):
    out = []
    for i in range(n):
        h = x.astype(bf)
        out.append(h)
        if i < n - 1:
            x = x - h.astype(f32)
    return out


TERMS = [(0, 0), (0, 1), (1, 0), (0, 2), (2, 0), (1, 1)]


def dots(a, b, nt):
    l = jnp.concatenate([a[i] for i, _ in TERMS], axis=1)
    r = jnp.concatenate([b[j] for _, j in TERMS], axis=1 if nt else 0)
    dims = (((1,), (1,) if nt else (0,)), ((), ()))
    return lax.dot_general(l, r, dims, preferred_element_type=f32)


def part(s, sl):
    return [x[sl] for x in s]


def leaf(a, G=16):
    nv=G//8; ng=B//G
    lane=lax.broadcasted_iota(jnp.int32,(8,B),1)
    sub=lax.broadcasted_iota(jnp.int32,(8,B),0)
    bl=lambda x,c: jnp.broadcast_to(x[:,c:c+1],(8,B))
    bs=lambda x,s: jnp.broadcast_to(x[s:s+1,:],(8,B))
    rows=[a[8*i:8*i+8,:] for i in range(16)]
    for g in range(ng):
        R=[rows[nv*g+v] for v in range(nv)]
        C=[[bl(R[v],G*g+c) for v in range(nv)] for c in range(G)]
        inb=(lane>=G*g)&(lane<G*g+G)
        RA=[jnp.where(inb, jnp.where(lane-G*g-8*v==sub,1.0,0.0), R[v]) for v in range(nv)]
        for j in range(0,G,2):
            jv,js=divmod(j,8)
            a0=bs(C[j][jv],js); b0=bs(C[j+1][jv],js); c0=bs(C[j+1][jv],js+1)
            r=pltpu.reciprocal(a0*c0-b0*b0,approx=True)
            u=[];w=[]
            for v in range(nv):
                cj,ck=C[j][v],C[j+1][v]
                if v==jv:
                    cj=jnp.where(sub==js,cj-1.0,cj); ck=jnp.where(sub==js+1,ck-1.0,ck)
                u.append(cj*c0-ck*b0); w.append(ck*a0-cj*b0)
            for c in range(j+2,G):
                x0=bs(C[c][jv],js); x1=bs(C[c][jv],js+1)
                for v in range(nv): C[c][v]=C[c][v]-(u[v]*x0+w[v]*x1)*r
            x0=bs(RA[jv],js); x1=bs(RA[jv],js+1)
            for v in range(nv): RA[v]=RA[v]-(u[v]*x0+w[v]*x1)*r
        new=list(rows)
        for v in range(nv): new[nv*g+v]=RA[v]
        near=[i for i in range(16) if i//nv==g+1]
        rb=[bs(RA[c//8],c%8) for c in range(G)] if near else []
        for i in near:
            p=[bl(rows[i],G*g+c)*rb[c] for c in range(G)]
            while len(p)>1: p=[p[2*k]+p[2*k+1] for k in range(len(p)//2)]
            new[i]=jnp.where(inb,0.0,rows[i])-p[0]
        rest=[i for i in range(16) if i//nv!=g and i not in near]
        zero=jnp.zeros((8,B),f32)
        d=lax.dot_general(jnp.concatenate([rows[i] for i in rest],0),
            jnp.concatenate([RA[i-nv*g] if i//nv==g else zero for i in range(16)],0),
            (((1,),(0,)),((),())),precision=lax.Precision.HIGHEST,preferred_element_type=f32)
        for m,i in enumerate(rest): new[i]=jnp.where(inb,0.0,rows[i])-d[8*m:8*m+8]
        rows=new
    return jnp.concatenate(rows,0)


class Links:
    def __init__(self, ssem, rsem):
        t, q = lax.axis_index("train"), lax.axis_index("query")
        self.y, self.z = t // NZ, lax.rem(t, NZ)
        self.x, self.c = q // 2, lax.rem(q, 2)
        self.ssem, self.rsem = ssem, rsem
        self.count = 0
        self.started = []

    def at(self, dx=0, dy=0, dz=0, dc=0):
        return (
            lax.rem(self.y + dy, NY) * NZ + lax.rem(self.z + dz, NZ),
            lax.rem(self.x + dx, NX) * 2 + lax.rem(self.c + dc, 2),
        )

    def send(self, src, dst, device):
        i = self.count
        self.count += 1
        copy = pltpu.make_async_remote_copy(
            src_ref=src, dst_ref=dst, send_sem=self.ssem.at[i], recv_sem=self.rsem.at[i],
            device_id=device, device_id_type=MESH)
        copy.start()
        self.started.append(copy)
        return copy


def arrive(copies):
    for copy in copies:
        copy.wait_recv()


def rows(base, i, size):
    return pl.ds(pl.multiple_of(base + i * size, 8), size)


def total_of(k, chunk, p_ref, o_ref, s1, w, sy, sz, sx):
    base, n = chunk
    h = n // 2
    u = h // NY
    t = u // NZ
    x, y, z, c = k.x, k.y, k.z, k.c
    a = [k.send(p_ref.at[rows(base, 1 - c, h)], s1, k.at(dc=1))]
    yield
    arrive(a)
    w[...] = p_ref[rows(base, c, h)] + s1[...]
    a = [k.send(w.at[rows(0, lax.rem(y + d, NY), u)], sy.at[d - 1], k.at(dy=d)) for d in (2, 1, 3)]
    yield
    arrive(a)
    sy[NY - 1] = (w[rows(0, y, u)] + sy[0]) + (sy[1] + sy[2])
    a = [k.send(sy.at[NY - 1, rows(0, lax.rem(z + d, NZ), t)], sz.at[d - 1], k.at(dz=d))
         for d in (4, 3, 5, 2, 6, 1, 7)]
    yield
    arrive(a)
    v = sy[NY - 1, rows(0, z, t)]
    for d in range(NZ - 1):
        v = v + sz[d]
    sx[NX - 1] = v
    a = [k.send(sx.at[NX - 1], sx.at[d - 1], k.at(dx=d)) for d in (2, 1, 3)]
    yield
    arrive(a)
    own = pl.ds(pl.multiple_of(base + c * h + y * u + z * t, 8), t)
    o_ref[own] = (sx[0] + sx[1]) + (sx[2] + sx[3])
    a = [k.send(o_ref.at[own], o_ref.at[own], k.at(dz=d)) for d in (4, 3, 5, 2, 6, 1, 7)]
    yield
    arrive(a)
    own = rows(base + c * h, y, u)
    a = [k.send(o_ref.at[own], o_ref.at[own], k.at(dy=d)) for d in (2, 1, 3)]
    yield
    arrive(a)
    own = rows(base, c, h)
    a = [k.send(o_ref.at[own], o_ref.at[own], k.at(dc=1))]
    yield
    arrive(a)
    yield


def chunk_scratch(chunk):
    h = chunk[1] // 2
    u = h // NY
    t = u // NZ
    shapes = [(h, B), (h, B), (NY, u, B), (NZ - 1, t, B), (NX, t, B)]
    return [pltpu.VMEM(s, f32) for s in shapes]


def gathered(k, x_ref, g_ref, own_sem):
    n = x_ref.shape[0]
    half = n // 2
    mine = (k.x * 2 + k.c) * n
    below, above = (lax.rem(k.x + NX - 1, NX) * 2 + k.c) * n, (lax.rem(k.x + 1, NX) * 2 + k.c) * n
    across = (lax.rem(k.x + 2, NX) * 2 + k.c) * n
    at = lambda base, first, size: g_ref.at[pl.ds(pl.multiple_of(base + first, 8), size)]
    own = pltpu.make_async_copy(x_ref, at(mine, 0, n), own_sem)
    own.start()
    src = [x_ref.at[pl.ds(i * half, half)] for i in range(2)]
    up = [k.send(src[0], at(mine, 0, half), k.at(dx=1))]
    down = [k.send(src[1], at(mine, half, half), k.at(dx=NX - 1))]
    yield
    up.append(k.send(src[1], at(mine, half, half), k.at(dx=1)))
    down.append(k.send(src[0], at(mine, 0, half), k.at(dx=NX - 1)))
    core = [k.send(x_ref, at(mine, 0, n), k.at(dc=1))]
    arrive([up[0], down[0]])
    lo, hi = at(below, 0, half), at(above, half, half)
    far = [k.send(lo, lo, k.at(dx=1)), k.send(hi, hi, k.at(dx=NX - 1))]
    yield
    arrive([up[1], down[1]])
    for base in (below, above):
        block = at(base, 0, n)
        core.append(k.send(block, block, k.at(dc=1)))
    yield
    arrive(far)
    block = at(across, 0, n)
    core.append(k.send(block, block, k.at(dc=1)))
    yield
    own.wait()
    arrive(core)
    yield


def kernel(total, x_hbm, q_hbm, o_ref, g_ref, x_ref, p_ref, f_ref, m_ref, b_ref, y0_ref, y1_ref, y2_ref,
           ssem, rsem, lsem, *scratch):
    y_refs = (y0_ref, y1_ref, y2_ref)
    k = Links(ssem, rsem)
    load = pltpu.make_async_copy(x_hbm, x_ref, lsem.at[0])
    load.start()
    q_load = pltpu.make_async_copy(q_hbm, b_ref, lsem.at[2])
    q_load.start()
    peers = [k.at(dc=1)] + [k.at(dx=d) for d in range(1, NX)]
    peers += [k.at(dy=d) for d in range(1, NY)] + [k.at(dz=d) for d in range(1, NZ)]
    barrier = pltpu.get_barrier_semaphore()
    for device in peers:
        pl.semaphore_signal(barrier, inc=1, device_id=device, device_id_type=MESH)
    load.wait()

    def gram(j):
        p_ref[OFF[j]:OFF[j + 1]] = lax.dot_general(
            x_ref[:, j * B:], x_ref[:, j * B:(j + 1) * B], (((0,), (0,)), ((), ())),
            precision=lax.Precision.HIGHEST, preferred_element_type=f32)

    row_at = lax.broadcasted_iota(jnp.int32, (B, B), 0)
    column_at = lax.broadcasted_iota(jnp.int32, (B, B), 1)
    corner = (row_at == 0) & (column_at == B - 1)
    eye = row_at == column_at
    squares = jnp.sum(x_ref[...] * x_ref[...], axis=0, keepdims=True) * (1.0 / total)
    gram(0)
    p_ref[:B] = jnp.where(corner, jnp.sum(squares, axis=1, keepdims=True), p_ref[:B])
    pl.semaphore_wait(barrier, len(peers))
    sums = [total_of(k, c, p_ref, f_ref, *scratch[5 * i:5 * i + 5]) for i, c in enumerate(CHUNKS)]
    gather = gathered(k, x_hbm, g_ref, lsem.at[1])
    done = [0] * len(sums)

    def go(*chunks):
        for i in chunks:
            next(sums[i])
            done[i] += 1

    go(0)
    next(gather)
    gram(1)
    gram(2)
    go(1, 0)
    for j in range(3, NB):
        gram(j)
    go(2, 3, 4, 1, 2, 3, 4)
    go(0, 1, 0, 2, 0, 1, 3, 4, 1, 2, 0, 2, 3, 4)
    next(gather)
    go(1, 3, 4, 0, 2, 0)
    d = f_ref[:B]
    trace = d[0:1, B - 1:B]
    damp = 0.1 * trace / K
    inv = 1.0 / damp
    scale = jnp.broadcast_to(inv * (1.0 / total), (1, B))
    d = jnp.where(corner, d[B - 1:B, 0:1], d) * scale
    dinv = leaf(jnp.where(eye, d + 1.0, d))
    q_load.wait()
    due = {0: (1, 3, 4, 1), 1: (2, 2), 2: (3, 4, 3, 4), 4: (-1,), 6: (-1,)}
    for i in range(NB):
        s, e = i * B, i * B + B
        left = (NB - 1 - i) * B
        ds = split(dinv)
        if i == NB - 1:
            b_ref[:, s:e] = dots(split(b_ref[:, s:e]), ds, False)
            break
        for j in due.get(i, ()):
            if j < 0:
                next(gather)
            else:
                go(j)
        first = i == 0
        a = f_ref[OFF[i] + B:OFF[i + 1]] * scale
        if not first:
            a = a + m_ref[OFF[i] + B:OFF[i + 1]]
        a = split(a)
        a1 = part(a, slice(0, B))
        y = split(dots(a1, ds, False))
        d = f_ref[OFF[i + 1]:OFF[i + 1] + B] * scale - dots(y, a1, True)
        d = jnp.where(eye, d + 1.0, d)
        if not first:
            d = d + m_ref[OFF[i + 1]:OFF[i + 1] + B]
        if i < NB - 2:
            y2 = split(dots(part(a, slice(B, left)), ds, False))

            def update(lo, hi, v):
                m_ref[lo:hi] = -v if first else m_ref[lo:hi] - v

            update(OFF[i + 1] + B, OFF[i + 2], dots(y2, a1, True))
            y = [jnp.concatenate([u, v], axis=0) for u, v in zip(y, y2)]
            for j in range(i + 2, NB, 2):
                at = (j - i - 1) * B
                wide = min(2, NB - j) * B
                v = dots(part(y, slice(at, left)), part(a, slice(at, at + wide)), True)
                update(OFF[j], OFF[j + 1], v[:, :B])
                if wide > B:
                    update(OFF[j + 1], OFF[j + 2], v[B:, B:])
        for r, v in zip(y_refs, y):
            r[OFF[i] + B:OFF[i + 1]] = v
        zed = dots(split(b_ref[:, s:e]), ds, False)
        b_ref[:, e:] -= dots(split(zed), a, True)
        b_ref[:, s:e] = zed
        dinv = leaf(d)
    for j in range(NB - 1, 0, -1):
        x = split(b_ref[:, j * B:(j + 1) * B])
        y = [jnp.concatenate([r[OFF[i] + (j - i) * B:OFF[i] + (j - i + 1) * B] for i in range(j)], axis=1)
             for r in y_refs]
        b_ref[:, :j * B] -= dots(x, y, False)
    next(gather)
    hi, lo = split(b_ref[...] * jnp.broadcast_to(inv * (1.0 / jnp.sqrt(f32(K))), (1, K)), 2)
    o_ref[:, :K] = hi
    o_ref[:, K:] = lo
    for copy in k.started:
        copy.wait_send()


def solve(train_grads, queries, total):
    nq, n = queries.shape[0], train_grads.shape[0]
    return pl.pallas_call(
        functools.partial(kernel, total),
        out_shape=[jax.ShapeDtypeStruct((nq, 2 * K), bf), jax.ShapeDtypeStruct((2 * NX * n, K), f32)],
        in_specs=[pl.BlockSpec(memory_space=pl.ANY)] * 2,
        out_specs=[pl.BlockSpec(memory_space=pltpu.VMEM), pl.BlockSpec(memory_space=pl.ANY)],
        scratch_shapes=[
            pltpu.VMEM((n, K), f32),
            pltpu.VMEM((OFF[NB], B), f32), pltpu.VMEM((OFF[NB], B), f32), pltpu.VMEM((OFF[NB], B), f32),
            pltpu.VMEM((nq, K), f32)] + [pltpu.VMEM((OFF[NB], B), bf)] * 3 + [
            pltpu.SemaphoreType.DMA((NCOPY,)), pltpu.SemaphoreType.DMA((NCOPY,)), pltpu.SemaphoreType.DMA((3,))]
        + [s for c in CHUNKS for s in chunk_scratch(c)],
        compiler_params=pltpu.CompilerParams(
            collective_id=0, has_side_effects=True, vmem_limit_bytes=60 * 2**20),
    )(train_grads, queries)


def scores_kernel(g_ref, x_ref, o_ref):
    hi, lo = split(g_ref[...], 2)
    left = jnp.concatenate([hi, lo, hi], axis=1)
    right = jnp.concatenate([x_ref[:, :K], x_ref[:, :K], x_ref[:, K:]], axis=1)
    o_ref[...] = lax.dot_general(left, right, (((1,), (1,)), ((), ())), preferred_element_type=f32)


def scores_of(g, x):
    n, nq = g.shape[0], x.shape[0]
    step = 1024
    return pl.pallas_call(
        scores_kernel,
        grid=(n // step,),
        out_shape=jax.ShapeDtypeStruct((n, nq), f32),
        in_specs=[pl.BlockSpec((step, K), lambda i: (i, 0)), pl.BlockSpec((nq, 2 * K), lambda i: (0, 0))],
        out_specs=pl.BlockSpec((step, nq), lambda i: (i, 0)),
        compiler_params=pltpu.CompilerParams(vmem_limit_bytes=60 * 2**20),
    )(g, x)


def local(train_grads, queries):
    total = train_grads.shape[0] * lax.axis_size("train") * lax.axis_size("query")
    precond, block = solve(train_grads, queries, float(total))
    return scores_of(block, precond)


def solution(mesh):
    in_specs = (P(("train", "query"), None), P("query", None))
    out_specs = P("train", "query")
    return jax.shard_map(local, mesh=mesh, in_specs=in_specs, out_specs=out_specs, check_vma=False)
```

time: 686 us -> 88.2 us (0.13)
  waiting for transfers between devices: 288 us -> 0 us
  other arithmetic: 263 us -> 0 us
  Pallas kernels: 0 us -> 88.1 us
  matrix products: 66.5 us -> 0 us
  local copies, waits for them, and re-layouts: 41.6 us -> 0 us
  between operations: 21.3 us -> 0.01 us
    psum x1 -> x0, waiting for transfers between devices: 287 us -> none  [local(): summed = lax.psum(operand, ('train', 'query'))]
    another operation x33 -> x0, other arithmetic: 251 us -> none  [the longest x30 167 us: precondition(): jnp.linalg.cholesky(fisher + damp * jnp.eye(width, dtype=fisher.dtype))]
    pallas_call x0 -> x2, Pallas kernels: none -> 88.1 us  [the longest x1 81 us: solve(): pl.pallas_call(functools.partial(kernel, total), out_shape=[jax.ShapeDtyp...]
    another operation x44 -> x0, matrix products: 43.6 us -> none  [the longest x14 25.9 us: precondition(): jnp.linalg.cholesky(fisher + damp * jnp.eye(width, dtype=fisher.dtype))]
    another operation x70 -> x0, local copies, waits for them, and re-layouts: 30.1 us -> none
    dot_general x2 -> x0, matrix products: 22.9 us -> none  [the longest x1 15.8 us: local(): jnp.dot(lax.all_gather(train_grads, 'query', axis=0, tiled=True), precond...]
  transfers between devices with their start and end apart: 2 -> 0, of which waited for: 1 -> 0; matrix products, arithmetic and copies ran while one was open for 50% -> 0% of each run, Pallas kernels for 0% -> 0%
where the time goes in v1:
time: 88.2 us; the launch traced here: 88.1 us
  Pallas kernels  88.1 us (100%)
    pallas_call x1, Pallas kernels, solve(): pl.pallas_call(functools.partial(kernel, total), out_shape=[jax.ShapeDtyp...  81 us
    pallas_call x1, Pallas kernels, scores_of(): pl.pallas_call(scores_kernel, grid=(n // step,), out_shape=jax.ShapeDtype...  7.16 us

profile of v1, /device:TPU:1, one launch (start us, length us, event | category | flops | bytes accessed | tf_op | source)
XLA Modules:
  0.0 88.1 jit_solution(6275228472723135189)
XLA Ops:
  0.0 81.0 %shard_map.28 = (bf16[256,2048]{1,0:T(8,128)(2,1)}, f32[2048,1024]{1,0:T(8,128)}) custom-call(f32[256,1024]{1,0:T(8,128)} %x_hbm.1, f32[256,1024]{1,0:T(8,128)} %q_hbm.1), custom_call_target="tpu_custom_call" | custom-call | tf_op jit(solution)/shard_map/pallas_call | solution.py:325
  81.0 7.2 %shard_map.29 = f32[2048,256]{1,0:T(8,128)} custom-call(f32[2048,1024]{1,0:T(8,128)} %get-tuple-element.7.g_ref, bf16[256,2048]{1,0:T(8,128)(2,1)} %get-tuple-element.8.x_ref), custom_call_target="tpu_custom_call" | custom-call | tf_op jit(solution)/shard_map/pallas_call | solution.py:351

commit v2 on v1

--- a/solution.py
+++ b/solution.py
@@ -14,9 +14,9 @@
 NY, NZ, NX = 4, 8, 4
 MESH = pl.DeviceIdType.MESH
 OFF = [sum((NB - i) * B for i in range(k)) for k in range(NB + 1)]
-CHUNKS = [(0, 1024), (1024, 1024), (2048, 1024), (3072, 1024), (4096, 512)]
-STAGES = 8
-NCOPY = 25 * len(CHUNKS) + 12
+CHUNKS = [(0, 512, "y"), (512, 1024, "y"), (1536, 1024, "y"), (2560, 1024, "y"), (3584, 1024, "y")]
+GATHER = -1
+NCOPY = 7 * len(CHUNKS) + 12
 
 
 def split(x, n=3):
@@ -119,56 +119,94 @@
         copy.wait_recv()
 
 
+class Exchange:
+    def __init__(self, k, whole, copies):
+        self.whole = whole
+        i = k.count
+        k.count += 1
+        self.ssem, self.rsem = k.ssem.at[i], k.rsem.at[i]
+        for src, dst, device in copies:
+            pltpu.make_async_remote_copy(
+                src_ref=src, dst_ref=dst, send_sem=self.ssem, recv_sem=self.rsem,
+                device_id=device, device_id_type=MESH).start()
+
+    def arrived(self):
+        pltpu.make_async_copy(self.whole, self.whole, self.rsem).wait()
+
+    def wait_send(self):
+        pltpu.make_async_copy(self.whole, self.whole, self.ssem).wait()
+
+
 def rows(base, i, size):
     return pl.ds(pl.multiple_of(base + i * size, 8), size)
 
 
-def total_of(k, chunk, p_ref, o_ref, s1, w, sy, sz, sx):
-    base, n = chunk
-    h = n // 2
-    u = h // NY
-    t = u // NZ
-    x, y, z, c = k.x, k.y, k.z, k.c
-    a = [k.send(p_ref.at[rows(base, 1 - c, h)], s1, k.at(dc=1))]
-    yield
-    arrive(a)
+def shares(chunk):
+    n1, n2 = (NY, NZ) if chunk[2] == "y" else (NZ, NY)
+    h = chunk[1] // 2
+    return n1, n2, h, h // n1, h // n1 // n2
+
+
+FAR_FIRST = {4: (2, 1, 3), 8: (4, 3, 5, 2, 6, 1, 7)}
+
+
+def total_of(k, chunk, p_ref, o_ref, s1, w, s2, s3, sx):
+    base = chunk[0]
+    n1, n2, h, u, t = shares(chunk)
+    c = k.c
+    if chunk[2] == "y":
+        i1, i2, to1, to2 = k.y, k.z, lambda d: k.at(dy=d), lambda d: k.at(dz=d)
+    else:
+        i1, i2, to1, to2 = k.z, k.y, lambda d: k.at(dz=d), lambda d: k.at(dy=d)
+    sent = [Exchange(k, s1, [(p_ref.at[rows(base, 1 - c, h)], s1, k.at(dc=1))])]
+    yield
+    sent[0].arrived()
     w[...] = p_ref[rows(base, c, h)] + s1[...]
-    a = [k.send(w.at[rows(0, lax.rem(y + d, NY), u)], sy.at[d - 1], k.at(dy=d)) for d in (2, 1, 3)]
-    yield
-    arrive(a)
-    sy[NY - 1] = (w[rows(0, y, u)] + sy[0]) + (sy[1] + sy[2])
-    a = [k.send(sy.at[NY - 1, rows(0, lax.rem(z + d, NZ), t)], sz.at[d - 1], k.at(dz=d))
-         for d in (4, 3, 5, 2, 6, 1, 7)]
-    yield
-    arrive(a)
-    v = sy[NY - 1, rows(0, z, t)]
-    for d in range(NZ - 1):
-        v = v + sz[d]
+    some2, some_x = s2.at[pl.ds(0, n1 - 1)], sx.at[pl.ds(0, NX - 1)]
+    sent.append(Exchange(k, some2, [
+        (w.at[rows(0, lax.rem(i1 + d, n1), u)], s2.at[d - 1], to1(d)) for d in FAR_FIRST[n1]]))
+    yield
+    sent[1].arrived()
+    v = w[rows(0, i1, u)]
+    for d in range(n1 - 1):
+        v = v + s2[d]
+    s2[n1 - 1] = v
+    sent.append(Exchange(k, s3, [
+        (s2.at[n1 - 1, rows(0, lax.rem(i2 + d, n2), t)], s3.at[d - 1], to2(d)) for d in FAR_FIRST[n2]]))
+    sent[0].wait_send()
+    yield
+    sent[2].arrived()
+    v = s2[n1 - 1, rows(0, i2, t)]
+    for d in range(n2 - 1):
+        v = v + s3[d]
     sx[NX - 1] = v
-    a = [k.send(sx.at[NX - 1], sx.at[d - 1], k.at(dx=d)) for d in (2, 1, 3)]
-    yield
-    arrive(a)
-    own = pl.ds(pl.multiple_of(base + c * h + y * u + z * t, 8), t)
+    sent.append(Exchange(k, some_x, [(sx.at[NX - 1], sx.at[d - 1], k.at(dx=d)) for d in FAR_FIRST[NX]]))
+    sent[1].wait_send()
+    yield
+    sent[3].arrived()
+    own = pl.ds(pl.multiple_of(base + c * h + i1 * u + i2 * t, 8), t)
     o_ref[own] = (sx[0] + sx[1]) + (sx[2] + sx[3])
-    a = [k.send(o_ref.at[own], o_ref.at[own], k.at(dz=d)) for d in (4, 3, 5, 2, 6, 1, 7)]
-    yield
-    arrive(a)
-    own = rows(base + c * h, y, u)
-    a = [k.send(o_ref.at[own], o_ref.at[own], k.at(dy=d)) for d in (2, 1, 3)]
-    yield
-    arrive(a)
+    sent.append(Exchange(k, s3, [(o_ref.at[own], o_ref.at[own], to2(d)) for d in FAR_FIRST[n2]]))
+    sent[2].wait_send()
+    yield
+    sent[4].arrived()
+    own = rows(base + c * h, i1, u)
+    sent.append(Exchange(k, some2, [(o_ref.at[own], o_ref.at[own], to1(d)) for d in FAR_FIRST[n1]]))
+    sent[3].wait_send()
+    yield
+    sent[5].arrived()
     own = rows(base, c, h)
-    a = [k.send(o_ref.at[own], o_ref.at[own], k.at(dc=1))]
-    yield
-    arrive(a)
+    sent.append(Exchange(k, s1, [(o_ref.at[own], o_ref.at[own], k.at(dc=1))]))
+    sent[4].wait_send()
+    yield
+    sent[6].arrived()
+    k.started += sent[5:]
     yield
 
 
 def chunk_scratch(chunk):
-    h = chunk[1] // 2
-    u = h // NY
-    t = u // NZ
-    shapes = [(h, B), (h, B), (NY, u, B), (NZ - 1, t, B), (NX, t, B)]
+    n1, n2, h, u, t = shares(chunk)
+    shapes = [(h, B), (h, B), (n1, u, B), (n2 - 1, t, B), (NX, t, B)]
     return [pltpu.VMEM(s, f32) for s in shapes]
 
 
@@ -222,9 +260,21 @@
     load.wait()
 
     def gram(j):
-        p_ref[OFF[j]:OFF[j + 1]] = lax.dot_general(
+        v = lax.dot_general(
             x_ref[:, j * B:], x_ref[:, j * B:(j + 1) * B], (((0,), (0,)), ((), ())),
             precision=lax.Precision.HIGHEST, preferred_element_type=f32)
+        if j == 0:
+            p_ref[:3 * B], p_ref[4 * B:9 * B] = v[:3 * B], v[3 * B:]
+        elif j == 1:
+            p_ref[3 * B:4 * B], p_ref[9 * B:15 * B] = v[:B], v[B:]
+        else:
+            p_ref[OFF[j]:OFF[j + 1]] = v
+
+    def top(j):
+        return f_ref[3 * B:4 * B] if j == 1 else f_ref[OFF[j]:OFF[j] + B]
+
+    def below(j):
+        return f_ref[OFF[j] + B:OFF[j + 1]]
 
     row_at = lax.broadcasted_iota(jnp.int32, (B, B), 0)
     column_at = lax.broadcasted_iota(jnp.int32, (B, B), 1)
@@ -232,6 +282,7 @@
     eye = row_at == column_at
     squares = jnp.sum(x_ref[...] * x_ref[...], axis=0, keepdims=True) * (1.0 / total)
     gram(0)
+    gram(1)
     p_ref[:B] = jnp.where(corner, jnp.sum(squares, axis=1, keepdims=True), p_ref[:B])
     pl.semaphore_wait(barrier, len(peers))
     sums = [total_of(k, c, p_ref, f_ref, *scratch[5 * i:5 * i + 5]) for i, c in enumerate(CHUNKS)]
@@ -245,15 +296,14 @@
 
     go(0)
     next(gather)
-    gram(1)
     gram(2)
     go(1, 0)
     for j in range(3, NB):
         gram(j)
     go(2, 3, 4, 1, 2, 3, 4)
-    go(0, 1, 0, 2, 0, 1, 3, 4, 1, 2, 0, 2, 3, 4)
+    go(0, 1, 0, 2, 0, 1, 4, 3, 1, 0, 2, 3, 2, 0, 4, 3)
     next(gather)
-    go(1, 3, 4, 0, 2, 0)
+    go(1, 0)
     d = f_ref[:B]
     trace = d[0:1, B - 1:B]
     damp = 0.1 * trace / K
@@ -262,7 +312,17 @@
     d = jnp.where(corner, d[B - 1:B, 0:1], d) * scale
     dinv = leaf(jnp.where(eye, d + 1.0, d))
     q_load.wait()
-    due = {0: (1, 3, 4, 1), 1: (2, 2), 2: (3, 4, 3, 4), 4: (-1,), 6: (-1,)}
+    at_start = {0: (2, 4), 1: (2, 4), 2: (3,), 4: (4, GATHER), 6: (GATHER,)}
+    at_next = {0: (1,), 1: (2,)}
+    at_leaf = {0: (3,), 1: (3,), 3: (4,)}
+
+    def advance(due):
+        for j in due:
+            if j == GATHER:
+                next(gather)
+            else:
+                go(j)
+
     for i in range(NB):
         s, e = i * B, i * B + B
         left = (NB - 1 - i) * B
@@ -270,29 +330,34 @@
         if i == NB - 1:
             b_ref[:, s:e] = dots(split(b_ref[:, s:e]), ds, False)
             break
-        for j in due.get(i, ()):
-            if j < 0:
-                next(gather)
-            else:
-                go(j)
-        first = i == 0
-        a = f_ref[OFF[i] + B:OFF[i + 1]] * scale
-        if not first:
-            a = a + m_ref[OFF[i] + B:OFF[i + 1]]
-        a = split(a)
-        a1 = part(a, slice(0, B))
-        y = split(dots(a1, ds, False))
-        d = f_ref[OFF[i + 1]:OFF[i + 1] + B] * scale - dots(y, a1, True)
-        d = jnp.where(eye, d + 1.0, d)
-        if not first:
-            d = d + m_ref[OFF[i + 1]:OFF[i + 1] + B]
+        advance(at_start.get(i, ()))
+        if i == 0:
+            a1 = split(f_ref[B:2 * B] * scale)
+            y = split(dots(a1, ds, False))
+            d = top(1) * scale - dots(y, a1, True)
+            advance(at_leaf[0])
+            dinv = leaf(jnp.where(eye, d + 1.0, d))
+            advance((1,))
+            zed = dots(split(b_ref[:, s:e]), ds, False)
+            advance(at_next[0])
+            a2 = split(jnp.concatenate([f_ref[2 * B:3 * B], f_ref[4 * B:9 * B]], axis=0) * scale)
+        else:
+            zed = dots(split(b_ref[:, s:e]), ds, False)
+            advance(at_next.get(i, ()))
+            a = split(below(i) * scale + m_ref[OFF[i] + B:OFF[i + 1]])
+            a1, a2 = part(a, slice(0, B)), part(a, slice(B, left))
+            y = split(dots(a1, ds, False))
+            v = dots(y, a1, True)
+            d = top(i + 1) * scale + (m_ref[OFF[i + 1]:OFF[i + 1] + B] - v)
+            d = jnp.where(eye, d + 1.0, d)
         if i < NB - 2:
-            y2 = split(dots(part(a, slice(B, left)), ds, False))
+            y2 = split(dots(a2, ds, False))
 
             def update(lo, hi, v):
-                m_ref[lo:hi] = -v if first else m_ref[lo:hi] - v
+                m_ref[lo:hi] = -v if i == 0 else m_ref[lo:hi] - v
 
             update(OFF[i + 1] + B, OFF[i + 2], dots(y2, a1, True))
+            a = [jnp.concatenate([u, v], axis=0) for u, v in zip(a1, a2)]
             y = [jnp.concatenate([u, v], axis=0) for u, v in zip(y, y2)]
             for j in range(i + 2, NB, 2):
                 at = (j - i - 1) * B
@@ -303,15 +368,18 @@
                     update(OFF[j + 1], OFF[j + 2], v[B:, B:])
         for r, v in zip(y_refs, y):
             r[OFF[i] + B:OFF[i + 1]] = v
-        zed = dots(split(b_ref[:, s:e]), ds, False)
         b_ref[:, e:] -= dots(split(zed), a, True)
         b_ref[:, s:e] = zed
-        dinv = leaf(d)
+        if i > 0:
+            advance(at_leaf.get(i, ()))
+            dinv = leaf(d)
     for j in range(NB - 1, 0, -1):
         x = split(b_ref[:, j * B:(j + 1) * B])
-        y = [jnp.concatenate([r[OFF[i] + (j - i) * B:OFF[i] + (j - i + 1) * B] for i in range(j)], axis=1)
-             for r in y_refs]
-        b_ref[:, :j * B] -= dots(x, y, False)
+        y = [[r[OFF[i] + (j - i) * B:OFF[i] + (j - i + 1) * B] for r in y_refs] for i in range(j)]
+        b_ref[:, (j - 1) * B:j * B] -= dots(x, y[j - 1], False)
+        if j > 1:
+            y = [jnp.concatenate([y[i][m] for i in range(j - 1)], axis=1) for m in range(3)]
+            b_ref[:, :(j - 1) * B] -= dots(x, y, False)
     next(gather)
     hi, lo = split(b_ref[...] * jnp.broadcast_to(inv * (1.0 / jnp.sqrt(f32(K))), (1, K)), 2)
     o_ref[:, :K] = hi

time: 88.2 us -> 83.9 us (0.951)
  Pallas kernels: 88.1 us -> 83.8 us
    pallas_call x1, Pallas kernels: 81 us -> 76.6 us  [solve(): pl.pallas_call(functools.partial(kernel, total), out_shape=[jax.ShapeDtyp...]
where the time goes in v2:
time: 83.9 us; the launch traced here: 83.8 us
  Pallas kernels  83.8 us (100%)
    pallas_call x1, Pallas kernels, solve(): pl.pallas_call(functools.partial(kernel, total), out_shape=[jax.ShapeDtyp...  76.6 us
    pallas_call x1, Pallas kernels, scores_of(): pl.pallas_call(scores_kernel, grid=(n // step,), out_shape=jax.ShapeDtype...  7.16 us

profile of v2, /device:TPU:1, one launch (start us, length us, event | category | flops | bytes accessed | tf_op | source)
XLA Modules:
  0.0 83.8 jit_solution(11344319073842936605)
XLA Ops:
  0.0 76.6 %shard_map.28 = (bf16[256,2048]{1,0:T(8,128)(2,1)}, f32[2048,1024]{1,0:T(8,128)}) custom-call(f32[256,1024]{1,0:T(8,128)} %x_hbm.1, f32[256,1024]{1,0:T(8,128)} %q_hbm.1), custom_call_target="tpu_custom_call" | custom-call | tf_op jit(solution)/shard_map/pallas_call | solution.py:393
  76.6 7.2 %shard_map.29 = f32[2048,256]{1,0:T(8,128)} custom-call(f32[2048,1024]{1,0:T(8,128)} %get-tuple-element.7.g_ref, bf16[256,2048]{1,0:T(8,128)(2,1)} %get-tuple-element.8.x_ref), custom_call_target="tpu_custom_call" | custom-call | tf_op jit(solution)/shard_map/pallas_call | solution.py:419

commit v3 on v2

--- a/solution.py
+++ b/solution.py
@@ -312,9 +312,9 @@
     d = jnp.where(corner, d[B - 1:B, 0:1], d) * scale
     dinv = leaf(jnp.where(eye, d + 1.0, d))
     q_load.wait()
-    at_start = {0: (2, 4), 1: (2, 4), 2: (3,), 4: (4, GATHER), 6: (GATHER,)}
-    at_next = {0: (1,), 1: (2,)}
-    at_leaf = {0: (3,), 1: (3,), 3: (4,)}
+    at_start = {0: (2,), 1: (2,), 2: (3, 4), 4: (4, GATHER), 6: (GATHER,)}
+    at_next = {0: (1,), 1: (2,), 2: (3,)}
+    at_leaf = {0: (1,), 3: (4,)}
 
     def advance(due):
         for j in due:
@@ -337,7 +337,7 @@
             d = top(1) * scale - dots(y, a1, True)
             advance(at_leaf[0])
             dinv = leaf(jnp.where(eye, d + 1.0, d))
-            advance((1,))
+            advance((3, 4))
             zed = dots(split(b_ref[:, s:e]), ds, False)
             advance(at_next[0])
             a2 = split(jnp.concatenate([f_ref[2 * B:3 * B], f_ref[4 * B:9 * B]], axis=0) * scale)

time: 83.9 us -> 83.8 us (level)
  no operation moved by 1% of the time
where the time goes in v3:
time: 83.8 us; the launch traced here: 83.7 us
  Pallas kernels  83.7 us (100%)
    pallas_call x1, Pallas kernels, solve(): pl.pallas_call(functools.partial(kernel, total), out_shape=[jax.ShapeDtyp...  76.5 us
    pallas_call x1, Pallas kernels, scores_of(): pl.pallas_call(scores_kernel, grid=(n // step,), out_shape=jax.ShapeDtype...  7.16 us

profile of v3, /device:TPU:1, one launch (start us, length us, event | category | flops | bytes accessed | tf_op | source)
XLA Modules:
  0.0 83.7 jit_solution(10564894807512200252)
XLA Ops:
  0.0 76.5 %shard_map.28 = (bf16[256,2048]{1,0:T(8,128)(2,1)}, f32[2048,1024]{1,0:T(8,128)}) custom-call(f32[256,1024]{1,0:T(8,128)} %x_hbm.1, f32[256,1024]{1,0:T(8,128)} %q_hbm.1), custom_call_target="tpu_custom_call" | custom-call | tf_op jit(solution)/shard_map/pallas_call | solution.py:393
  76.5 7.2 %shard_map.29 = f32[2048,256]{1,0:T(8,128)} custom-call(f32[2048,1024]{1,0:T(8,128)} %get-tuple-element.7.g_ref, bf16[256,2048]{1,0:T(8,128)(2,1)} %get-tuple-element.8.x_ref), custom_call_target="tpu_custom_call" | custom-call | tf_op jit(solution)/shard_map/pallas_call | solution.py:419
